TPU v7x, 512 devices: a whole 4x4x16 slice. The times are simulated.
512 devices in a mesh: tok: 16 (over z), col: 32 (over x, y, core).
Axes of the slice: x: 4, y: 4, z: 16, core: 2. Of those that a mesh axis runs over, the one named last changes fastest.
Arguments:
- acts: bfloat16 [8192, 28672], P('tok', 'col'), may hold values from -6 to 6
- residual: float32 [8192, 8192], P('tok', 'col'), may hold values from -6 to 6
- weights: bfloat16 [32, 896, 8192], P(None, 'tok', 'col'), may hold values from -6 to 6
- order: int32 [4], replicated, may hold values from 0 to 31
- rate: float32 [32], replicated, may hold values from 0.1 to 0.4
- penalty: float32 [32], replicated, may hold values from 0.4 to 1.2
Outputs:
- pruned: float32 [32, 896, 8192], P(None, 'tok', 'col')
- resid_out: float32 [8192, 8192], P('tok', 'col')
Inputs may be any that keep to these rules, and one draw needn't show every extreme that they name: `order`: block indices, repeats allowed.
All inputs are finite; a program needn't handle non-finite values.
Results may differ from a plain program's by a relative error of at most 0.0054.
Values may be sent and summed in bfloat16 or wider, within the bound.
A program may use at most 64 MiB of HBM per device.

v0:
```python
import math
import jax
import jax.numpy as jnp
from jax import lax
from jax.sharding import PartitionSpec as P

D = 8192
CH = 28672
STEPS = 4


def from_root(block, axis, holder):
    block = jnp.where(lax.axis_index(axis) == holder, block, jnp.zeros_like(block))
    return lax.psum(block, axis)


def body(acts, residual, weights, order, rate, penalty):
    tok_rows = acts.shape[0]
    scale = math.sqrt(CH)
    thresh_unit = math.sqrt(D)
    eta_unit = float(CH) / float(tok_rows * lax.axis_size("tok"))
    state = weights.astype(jnp.float32)
    resid = residual
    for step in range(STEPS):
        which = order[step]
        block_acts = from_root(acts, "col", which)
        lowered = resid.astype(jnp.bfloat16)
        partial_grad = lax.dot_general(
            block_acts, lowered, (((0,), (0,)), ((), ())), preferred_element_type=jnp.float32
        )
        current = lax.dynamic_index_in_dim(state, which, 0, keepdims=False)
        step_size = rate[which] * eta_unit
        limit = penalty[which] * thresh_unit
        grad = lax.psum_scatter(partial_grad, "tok", scatter_dimension=0, tiled=True) / scale
        shifted = current - step_size * grad
        sums = lax.psum(jnp.sum(shifted * shifted, axis=1), "col")
        factor = jnp.maximum(0.0, 1.0 - limit / jnp.sqrt(sums + 1e-06))
        fresh = factor[:, None] * shifted
        local_change = (fresh - current).astype(jnp.bfloat16)
        state = lax.dynamic_update_index_in_dim(state, fresh, which, 0)
        change = lax.all_gather(local_change, "tok", axis=0, tiled=True)
        resid = resid + jnp.dot(block_acts, change, preferred_element_type=jnp.float32) / scale
    return (state, resid)


def solution(mesh):
    in_specs = (P("tok", "col"), P("tok", "col"), P(None, "tok", "col"), P(), P(), P())
    out_specs = (P(None, "tok", "col"), P("tok", "col"))
    return jax.shard_map(body, mesh=mesh, in_specs=in_specs, out_specs=out_specs, check_vma=False)
```

profile of v0, /device:TPU:32, one launch (start us, length us, event | category | flops | bytes accessed | tf_op | source)
XLA Modules:
  0.0 816.7 jit_solution(8121737015502011051)
XLA Ops:
  7.2 1.4 fusion.18
  11.1 3.1 broadcast_select_fusion
  14.3 145.9 %all-reduce.3.cloned.1.call-done = (bf16[512,896]{1,0:T(8,128)(2,1)}, bf16[512,896]{1,0:T(8,128)(2,1)}, bf16[512,896]{1,0:T(8,128)(2,1)}, bf16[512,896]{1,0:T(8,128)(2,1)}) async-done(((bf16[512,896]{1,0:T(8,128)(2,1)}, bf16[512,896]{1,0:T(8,128)(2,1)}, bf16[512,896]{1,0:T(8,128)(2,1)}, bf16[512,896]{1,0:T(8,128)(2,1)}), (bf16[512,896]{1,0:T(8,128)(2,1)}, bf16[512,896]{1,0:T(8,128)(2,1)}, ...) | async-done | bytes 3670032 | tf_op jit(solution)/shard_map/psum | solution.py:14
  160.2 2.5 fusion.10
  167.8 1.4 convert_element_type.27
  174.4 57.9 %reduce-scatter.5.cloned.1.call-done = f32[56,256]{1,0:T(8,128)} async-done(((f32[896,256]{1,0:T(8,128)}), f32[56,256]{1,0:T(8,128)}) %reduce-scatter.5.cloned.1.call-update) | async-done | bytes 57360 | tf_op jit(solution)/shard_map/reduce_scatter | solution.py:34
  232.3 1.0 multiply_reduce_fusion.3
  233.2 62.7 %psum.57 = f32[56]{0:T(128)S(1)} all-reduce(f32[56]{0:T(128)S(1)} %get-tuple-element.12), channel_id=1, replica_groups=mesh['tok'=16,'col'=32] {'col'}, use_global_device_ids=true, to_apply=%region_3.4 | all-reduce | flops 56 | bytes 448 | tf_op jit(solution)/shard_map/psum | solution.py:36
  295.9 0.9 fusion.15
  296.8 29.3 %all_gather.12 = bf16[896,256]{1,0:T(8,128)(2,1)S(1)} all-gather(bf16[56,256]{1,0:T(8,128)(2,1)S(1)} %fusion.15), channel_id=1, replica_groups=mesh['tok'=16,'col'=32] {'tok'}, dimensions={0}, use_global_device_ids=true | all-gather | bytes 487424 | tf_op jit(solution)/shard_map/all_gather | solution.py:41
  326.6 1.4 fusion.8
  329.3 0.7 bitcast_dynamic-update-slice_fusion.3
  330.0 62.9 %reduce-scatter.7.cloned.1.call-done = f32[56,256]{1,0:T(8,128)} async-done(((f32[896,256]{1,0:T(8,128)}), f32[56,256]{1,0:T(8,128)}) %reduce-scatter.7.cloned.1.call-update) | async-done | bytes 57360 | tf_op jit(solution)/shard_map/reduce_scatter | solution.py:34
  392.9 1.0 multiply_reduce_fusion.2
  393.8 62.7 %psum.59 = f32[56]{0:T(128)S(1)} all-reduce(f32[56]{0:T(128)S(1)} %get-tuple-element.10), channel_id=1, replica_groups=mesh['tok'=16,'col'=32] {'col'}, use_global_device_ids=true, to_apply=%region_7.8 | all-reduce | flops 56 | bytes 448 | tf_op jit(solution)/shard_map/psum | solution.py:36
  456.5 0.9 fusion.14
  457.4 29.4 %all_gather.13 = bf16[896,256]{1,0:T(8,128)(2,1)S(1)} all-gather(bf16[56,256]{1,0:T(8,128)(2,1)S(1)} %fusion.14), channel_id=1, replica_groups=mesh['tok'=16,'col'=32] {'tok'}, dimensions={0}, use_global_device_ids=true | all-gather | bytes 487424 | tf_op jit(solution)/shard_map/all_gather | solution.py:41
  487.3 1.4 fusion.6
  490.2 0.7 bitcast_dynamic-update-slice_fusion.2
  490.9 62.7 %reduce-scatter.9.cloned.1.call-done = f32[56,256]{1,0:T(8,128)} async-done(((f32[896,256]{1,0:T(8,128)}), f32[56,256]{1,0:T(8,128)}) %reduce-scatter.9.cloned.1.call-update) | async-done | bytes 57360 | tf_op jit(solution)/shard_map/reduce_scatter | solution.py:34
  553.6 1.0 multiply_reduce_fusion.1
  554.5 62.7 %psum.61 = f32[56]{0:T(128)S(1)} all-reduce(f32[56]{0:T(128)S(1)} %get-tuple-element.8), channel_id=1, replica_groups=mesh['tok'=16,'col'=32] {'col'}, use_global_device_ids=true, to_apply=%region_11.12 | all-reduce | flops 56 | bytes 448 | tf_op jit(solution)/shard_map/psum | solution.py:36
  617.2 0.9 fusion.13
  618.1 29.4 %all_gather.14 = bf16[896,256]{1,0:T(8,128)(2,1)S(1)} all-gather(bf16[56,256]{1,0:T(8,128)(2,1)S(1)} %fusion.13), channel_id=1, replica_groups=mesh['tok'=16,'col'=32] {'tok'}, dimensions={0}, use_global_device_ids=true | all-gather | bytes 487424 | tf_op jit(solution)/shard_map/all_gather | solution.py:41
  648.0 1.4 fusion.4
  650.7 0.7 bitcast_dynamic-update-slice_fusion.1
  651.4 62.8 %reduce-scatter.11.cloned.1.call-done = f32[56,256]{1,0:T(8,128)} async-done(((f32[896,256]{1,0:T(8,128)}), f32[56,256]{1,0:T(8,128)}) %reduce-scatter.11.cloned.1.call-update) | async-done | bytes 57360 | tf_op jit(solution)/shard_map/reduce_scatter | solution.py:34
  714.2 1.0 multiply_reduce_fusion
  715.2 62.7 %psum.63 = f32[56]{0:T(128)S(1)} all-reduce(f32[56]{0:T(128)S(1)} %get-tuple-element.6), channel_id=1, replica_groups=mesh['tok'=16,'col'=32] {'col'}, use_global_device_ids=true, to_apply=%region_15.16 | all-reduce | flops 56 | bytes 448 | tf_op jit(solution)/shard_map/psum | solution.py:36
  777.9 0.9 fusion.12
  779.5 29.4 %all_gather.15 = bf16[896,256]{1,0:T(8,128)(2,1)S(1)} all-gather(bf16[56,256]{1,0:T(8,128)(2,1)S(1)} %fusion.12), channel_id=1, replica_groups=mesh['tok'=16,'col'=32] {'tok'}, dimensions={0}, use_global_device_ids=true | all-gather | bytes 487424 | tf_op jit(solution)/shard_map/all_gather | solution.py:41
  808.9 1.2 fusion.3
  (36 shorter events, 3.7 us)
Async XLA Ops:
  7.2 153.0 %all-reduce.3.cloned.1.call-start = ((), (), s32[]{:S(2)}) async-start(), calls=%async_computation.8 | async-start | bytes 7340032 | tf_op jit(solution)/shard_map/psum | solution.py:14
  14.2 146.0 %copy-start.4 = (f32[512,256]{1,0:T(8,128)S(1)}, f32[512,256]{1,0:T(8,128)}, u32[]{:S(2)}) copy-start(f32[512,256]{1,0:T(8,128)} %param.7) | copy-start | bytes 1572868
  14.2 153.5 %copy-start.5 = (bf16[32,56,256]{2,1,0:T(8,128)(2,1)S(1)}, bf16[32,56,256]{2,1,0:T(8,128)(2,1)}, u32[]{:S(2)}) copy-start(bf16[32,56,256]{2,1,0:T(8,128)(2,1)} %param.8) | copy-start | bytes 2752516
  14.3 218.0 %reduce-scatter.5.cloned.1.call-start = ((), (), s32[]{:S(2)}) async-start(), calls=%async_computation.4 | async-start | bytes 974848 | tf_op jit(solution)/shard_map/reduce_scatter | solution.py:34
  162.7 9.0 %copy-start.6 = (f32[32]{0:T(128)S(1)}, f32[32]{0:T(128)}, u32[]{:S(2)}) copy-start(f32[32]{0:T(128)} %param.10) | copy-start | bytes 388
  162.7 10.3 %copy-start.7 = (f32[32]{0:T(128)S(1)}, f32[32]{0:T(128)}, u32[]{:S(2)}) copy-start(f32[32]{0:T(128)} %param.11) | copy-start | bytes 388
  162.7 163.4 %copy-start.3 = (bf16[512,896]{1,0:T(8,128)(2,1)S(1)}, bf16[512,896]{1,0:T(8,128)(2,1)}, u32[]{:S(2)}) copy-start(bf16[512,896]{1,0:T(8,128)(2,1)} %get-tuple-element.2) | copy-start | bytes 2752516
  162.8 230.1 %reduce-scatter.7.cloned.1.call-start = ((), (), s32[]{:S(2)}) async-start(), calls=%async_computation.5 | async-start | bytes 974848 | tf_op jit(solution)/shard_map/reduce_scatter | solution.py:34
  169.2 157.5 %copy-start.2 = (bf16[512,896]{1,0:T(8,128)(2,1)S(1)}, bf16[512,896]{1,0:T(8,128)(2,1)}, u32[]{:S(2)}) copy-start(bf16[512,896]{1,0:T(8,128)(2,1)} %get-tuple-element.3) | copy-start | bytes 2752516
  328.0 159.3 %copy-start.1 = (bf16[512,896]{1,0:T(8,128)(2,1)S(1)}, bf16[512,896]{1,0:T(8,128)(2,1)}, u32[]{:S(2)}) copy-start(bf16[512,896]{1,0:T(8,128)(2,1)} %get-tuple-element.4) | copy-start | bytes 2752516
  328.0 225.6 %reduce-scatter.9.cloned.1.call-start = ((), (), s32[]{:S(2)}) async-start(), calls=%async_computation.6 | async-start | bytes 974848 | tf_op jit(solution)/shard_map/reduce_scatter | solution.py:34
  488.8 159.3 %copy-start = (bf16[512,896]{1,0:T(8,128)(2,1)S(1)}, bf16[512,896]{1,0:T(8,128)(2,1)}, u32[]{:S(2)}) copy-start(bf16[512,896]{1,0:T(8,128)(2,1)} %get-tuple-element.5) | copy-start | bytes 2752516
  488.8 225.5 %reduce-scatter.11.cloned.1.call-start = ((), (), s32[]{:S(2)}) async-start(), calls=%async_computation.7 | async-start | bytes 974848 | tf_op jit(solution)/shard_map/reduce_scatter | solution.py:34
Sparse Core Ops, SparseCore 0:
  14.4 145.7 all-reduce.2
  163.0 69.2 reduce-scatter.4
  328.1 64.6 reduce-scatter.6
  488.9 64.6 reduce-scatter.8
  649.6 64.6 reduce-scatter.10
where the time goes:
time: 818 us; the launch traced here: 817 us
  waiting for transfers between devices  392 us (48%)
  blocking collectives  368 us (45%)
  between operations  29 us (4%)
  other arithmetic  14.8 us (2%)
  matrix products  9.26 us (1%)
    psum x4, blocking collectives, body(): sums = lax.psum(jnp.sum(shifted * shifted, axis=1), 'col')  251 us
    reduce_scatter x4, waiting for transfers between devices, body(): lax.psum_scatter(partial_grad, 'tok', scatter_dimension=0, tiled=True)  246 us
    psum x1, waiting for transfers between devices, from_root(): return lax.psum(block, axis)  146 us
    all_gather x4, blocking collectives, body(): change = lax.all_gather(local_change, 'tok', axis=0, tiled=True)  118 us
  transfers between devices with their start and end apart: 5, of which 5 were waited for; matrix products, arithmetic and copies ran while one was open for 1% of the time, Pallas kernels for 0%

commit v1 on v0

--- a/solution.py
+++ b/solution.py
@@ -38,7 +38,9 @@
         fresh = factor[:, None] * shifted
         local_change = (fresh - current).astype(jnp.bfloat16)
         state = lax.dynamic_update_index_in_dim(state, fresh, which, 0)
-        change = lax.all_gather(local_change, "tok", axis=0, tiled=True)
+        ready = jnp.stack([local_change for _ in range(jax.lax.psum(1, "tok"))])
+        then = jax.lax.all_to_all(ready, "tok", 0, 0)
+        change = jnp.concatenate(then, axis=0)
         resid = resid + jnp.dot(block_acts, change, preferred_element_type=jnp.float32) / scale
     return (state, resid)
 

time: 818 us -> 827 us (1.011)
  the two profiles are of different devices: /device:TPU:32 before, /device:TPU:96 now
where the time goes in v1:
time: 827 us; the launch traced here: 826 us
  waiting for transfers between devices  405 us (49%)
  blocking collectives  355 us (43%)
  between operations  28.8 us (3%)
  other arithmetic  14.8 us (2%)
  starting transfers between devices  9.51 us (1%)
  matrix products  9.25 us (1%)
    psum x4, blocking collectives, body(): sums = lax.psum(jnp.sum(shifted * shifted, axis=1), 'col')  251 us
    reduce_scatter x4, waiting for transfers between devices, body(): lax.psum_scatter(partial_grad, 'tok', scatter_dimension=0, tiled=True)  235 us
    psum x1, waiting for transfers between devices, from_root(): return lax.psum(block, axis)  145 us
    all_to_all x3, blocking collectives, body(): then = jax.lax.all_to_all(ready, 'tok', 0, 0)  105 us
    all_to_all x1, waiting for transfers between devices, body(): then = jax.lax.all_to_all(ready, 'tok', 0, 0)  25 us
  transfers between devices with their start and end apart: 6, of which 6 were waited for; matrix products, arithmetic and copies ran while one was open for 1% of the time, Pallas kernels for 0%

profile of v1, /device:TPU:96, one launch (start us, length us, event | category | flops | bytes accessed | tf_op | source)
XLA Modules:
  0.0 826.2 jit_solution(7199961685100313640)
XLA Ops:
  7.2 1.4 fusion.18
  11.1 3.1 broadcast_select_fusion
  14.3 145.1 %all-reduce.3.cloned.1.call-done = (bf16[512,896]{1,0:T(8,128)(2,1)}, bf16[512,896]{1,0:T(8,128)(2,1)}, bf16[512,896]{1,0:T(8,128)(2,1)}, bf16[512,896]{1,0:T(8,128)(2,1)}) async-done(((bf16[512,896]{1,0:T(8,128)(2,1)}, bf16[512,896]{1,0:T(8,128)(2,1)}, bf16[512,896]{1,0:T(8,128)(2,1)}, bf16[512,896]{1,0:T(8,128)(2,1)}), (bf16[512,896]{1,0:T(8,128)(2,1)}, bf16[512,896]{1,0:T(8,128)(2,1)}, ...) | async-done | bytes 3670032 | tf_op jit(solution)/shard_map/psum | solution.py:14
  159.4 2.5 fusion.10
  167.0 1.4 convert_element_type.27
  173.5 58.2 %reduce-scatter.5.cloned.1.call-done = f32[56,256]{1,0:T(8,128)} async-done(((f32[896,256]{1,0:T(8,128)}), f32[56,256]{1,0:T(8,128)}) %reduce-scatter.5.cloned.1.call-update) | async-done | bytes 57360 | tf_op jit(solution)/shard_map/reduce_scatter | solution.py:34
  231.7 1.0 multiply_reduce_fusion.3
  232.7 62.7 %psum.57 = f32[56]{0:T(128)S(1)} all-reduce(f32[56]{0:T(128)S(1)} %get-tuple-element.12), channel_id=1, replica_groups=mesh['tok'=16,'col'=32] {'col'}, use_global_device_ids=true, to_apply=%region_3.4 | all-reduce | flops 56 | bytes 448 | tf_op jit(solution)/shard_map/psum | solution.py:36
  295.3 0.9 fusion.15
  296.3 34.9 %all_to_all.20 = bf16[16,56,256]{2,1,0:T(8,128)(2,1)S(1)} all-to-all(bf16[16,56,256]{2,1,0:T(8,128)(2,1)S(1)} %stack.8), channel_id=1, replica_groups=mesh['tok'=16,'col'=32] {'tok'}, dimensions={0} | all-to-all | bytes 917504 | tf_op jit(solution)/shard_map/all_to_all | solution.py:42
  331.7 1.4 fusion.8
  334.2 0.7 bitcast_dynamic-update-slice_fusion.3
  334.9 58.9 %reduce-scatter.7.cloned.1.call-done = f32[56,256]{1,0:T(8,128)} async-done(((f32[896,256]{1,0:T(8,128)}), f32[56,256]{1,0:T(8,128)}) %reduce-scatter.7.cloned.1.call-update) | async-done | bytes 57360 | tf_op jit(solution)/shard_map/reduce_scatter | solution.py:34
  393.8 1.0 multiply_reduce_fusion.2
  394.8 62.7 %psum.59 = f32[56]{0:T(128)S(1)} all-reduce(f32[56]{0:T(128)S(1)} %get-tuple-element.10), channel_id=1, replica_groups=mesh['tok'=16,'col'=32] {'col'}, use_global_device_ids=true, to_apply=%region_7.8 | all-reduce | flops 56 | bytes 448 | tf_op jit(solution)/shard_map/psum | solution.py:36
  457.5 0.9 fusion.14
  458.4 34.9 %all_to_all.21 = bf16[16,56,256]{2,1,0:T(8,128)(2,1)S(1)} all-to-all(bf16[16,56,256]{2,1,0:T(8,128)(2,1)S(1)} %stack.9), channel_id=1, replica_groups=mesh['tok'=16,'col'=32] {'tok'}, dimensions={0} | all-to-all | bytes 917504 | tf_op jit(solution)/shard_map/all_to_all | solution.py:42
  493.8 1.4 fusion.6
  497.3 58.7 %reduce-scatter.9.cloned.1.call-done = f32[56,256]{1,0:T(8,128)} async-done(((f32[896,256]{1,0:T(8,128)}), f32[56,256]{1,0:T(8,128)}) %reduce-scatter.9.cloned.1.call-update) | async-done | bytes 57360 | tf_op jit(solution)/shard_map/reduce_scatter | solution.py:34
  556.0 1.0 multiply_reduce_fusion.1
  557.0 62.7 %psum.61 = f32[56]{0:T(128)S(1)} all-reduce(f32[56]{0:T(128)S(1)} %get-tuple-element.8), channel_id=1, replica_groups=mesh['tok'=16,'col'=32] {'col'}, use_global_device_ids=true, to_apply=%region_11.12 | all-reduce | flops 56 | bytes 448 | tf_op jit(solution)/shard_map/psum | solution.py:36
  619.7 0.9 fusion.13
  620.6 34.9 %all_to_all.22 = bf16[16,56,256]{2,1,0:T(8,128)(2,1)S(1)} all-to-all(bf16[16,56,256]{2,1,0:T(8,128)(2,1)S(1)} %stack.10), channel_id=1, replica_groups=mesh['tok'=16,'col'=32] {'tok'}, dimensions={0} | all-to-all | bytes 917504 | tf_op jit(solution)/shard_map/all_to_all | solution.py:42
  656.0 1.4 fusion.4
  659.4 58.8 %reduce-scatter.11.cloned.1.call-done = f32[56,256]{1,0:T(8,128)} async-done(((f32[896,256]{1,0:T(8,128)}), f32[56,256]{1,0:T(8,128)}) %reduce-scatter.11.cloned.1.call-update) | async-done | bytes 57360 | tf_op jit(solution)/shard_map/reduce_scatter | solution.py:34
  718.2 1.0 multiply_reduce_fusion
  719.1 62.7 %psum.63 = f32[56]{0:T(128)S(1)} all-reduce(f32[56]{0:T(128)S(1)} %get-tuple-element.6), channel_id=1, replica_groups=mesh['tok'=16,'col'=32] {'col'}, use_global_device_ids=true, to_apply=%region_15.16 | all-reduce | flops 56 | bytes 448 | tf_op jit(solution)/shard_map/psum | solution.py:36
  781.8 0.9 fusion.12
  782.7 0.8 stack.11
  783.5 9.3 %all-to-all-start.3 = ((bf16[16,56,256]{2,1,0:T(8,128)(2,1)}), bf16[16,56,256]{2,1,0:T(8,128)(2,1)S(1)}, u32[]{:S(2)}, u32[]{:S(2)}) async-start(bf16[16,56,256]{2,1,0:T(8,128)(2,1)} %stack.11), calls=%async_computation.7 | async-start | bytes 917504 | tf_op jit(solution)/shard_map/all_to_all | solution.py:42
  793.5 25.0 %all-to-all-done.3 = bf16[16,56,256]{2,1,0:T(8,128)(2,1)S(1)} async-done(((bf16[16,56,256]{2,1,0:T(8,128)(2,1)}), bf16[16,56,256]{2,1,0:T(8,128)(2,1)S(1)}, u32[]{:S(2)}, u32[]{:S(2)}) %all-to-all-start.3) | async-done | bytes 458784 | tf_op jit(solution)/shard_map/all_to_all | solution.py:42
  818.5 1.2 fusion.3
  (41 shorter events, 5.2 us)
Async XLA Ops:
  7.2 152.3 %all-reduce.3.cloned.1.call-start = ((), (), s32[]{:S(2)}) async-start(), calls=%async_computation.12 | async-start | bytes 7340032 | tf_op jit(solution)/shard_map/psum | solution.py:14
  14.2 145.2 %copy-start.4 = (f32[512,256]{1,0:T(8,128)S(1)}, f32[512,256]{1,0:T(8,128)}, u32[]{:S(2)}) copy-start(f32[512,256]{1,0:T(8,128)} %param.7) | copy-start | bytes 1572868
  14.2 152.7 %copy-start.5 = (bf16[32,56,256]{2,1,0:T(8,128)(2,1)S(1)}, bf16[32,56,256]{2,1,0:T(8,128)(2,1)}, u32[]{:S(2)}) copy-start(bf16[32,56,256]{2,1,0:T(8,128)(2,1)} %param.8) | copy-start | bytes 2752516
  14.3 217.4 %reduce-scatter.5.cloned.1.call-start = ((), (), s32[]{:S(2)}) async-start(), calls=%async_computation.8 | async-start | bytes 974848 | tf_op jit(solution)/shard_map/reduce_scatter | solution.py:34
  162.0 8.8 %copy-start.6 = (f32[32]{0:T(128)S(1)}, f32[32]{0:T(128)}, u32[]{:S(2)}) copy-start(f32[32]{0:T(128)} %param.10) | copy-start | bytes 388
  162.0 10.1 %copy-start.7 = (f32[32]{0:T(128)S(1)}, f32[32]{0:T(128)}, u32[]{:S(2)}) copy-start(f32[32]{0:T(128)} %param.11) | copy-start | bytes 388
  162.0 231.8 %reduce-scatter.7.cloned.1.call-start = ((), (), s32[]{:S(2)}) async-start(), calls=%async_computation.9 | async-start | bytes 974848 | tf_op jit(solution)/shard_map/reduce_scatter | solution.py:34
  167.0 164.2 %copy-start.3 = (bf16[512,896]{1,0:T(8,128)(2,1)S(1)}, bf16[512,896]{1,0:T(8,128)(2,1)}, u32[]{:S(2)}) copy-start(bf16[512,896]{1,0:T(8,128)(2,1)} %get-tuple-element.2) | copy-start | bytes 2752516
  296.3 35.4 %copy-start.2 = (bf16[512,896]{1,0:T(8,128)(2,1)S(1)}, bf16[512,896]{1,0:T(8,128)(2,1)}, u32[]{:S(2)}) copy-start(bf16[512,896]{1,0:T(8,128)(2,1)} %get-tuple-element.3) | copy-start | bytes 2752516
  333.1 222.9 %reduce-scatter.9.cloned.1.call-start = ((), (), s32[]{:S(2)}) async-start(), calls=%async_computation.10 | async-start | bytes 974848 | tf_op jit(solution)/shard_map/reduce_scatter | solution.py:34
  458.4 35.4 %copy-start.1 = (bf16[512,896]{1,0:T(8,128)(2,1)S(1)}, bf16[512,896]{1,0:T(8,128)(2,1)}, u32[]{:S(2)}) copy-start(bf16[512,896]{1,0:T(8,128)(2,1)} %get-tuple-element.4) | copy-start | bytes 2752516
  495.2 222.9 %reduce-scatter.11.cloned.1.call-start = ((), (), s32[]{:S(2)}) async-start(), calls=%async_computation.11 | async-start | bytes 974848 | tf_op jit(solution)/shard_map/reduce_scatter | solution.py:34
  620.6 35.4 %copy-start = (bf16[512,896]{1,0:T(8,128)(2,1)S(1)}, bf16[512,896]{1,0:T(8,128)(2,1)}, u32[]{:S(2)}) copy-start(bf16[512,896]{1,0:T(8,128)(2,1)} %get-tuple-element.5) | copy-start | bytes 2752516
  783.5 35.0 %all-to-all-start.3 = ((bf16[16,56,256]{2,1,0:T(8,128)(2,1)}), bf16[16,56,256]{2,1,0:T(8,128)(2,1)S(1)}, u32[]{:S(2)}, u32[]{:S(2)}) async-start(bf16[16,56,256]{2,1,0:T(8,128)(2,1)} %stack.11), calls=%async_computation.7 | async-start | bytes 917504 | tf_op jit(solution)/shard_map/all_to_all | solution.py:42
Sparse Core Ops, SparseCore 0:
  14.4 145.0 all-reduce.2
  162.2 69.4 reduce-scatter.4
  333.2 60.5 reduce-scatter.6
  495.4 60.6 reduce-scatter.8
  657.5 60.6 reduce-scatter.10
